TPU v7x, 256 devices: a whole 4x4x8 slice. The times are simulated.
256 devices in a mesh: size: 4 (over x_hi, core), gz: 64 (over z, y, x_lo).
Axes of the slice: x: 4 (x_hi: 2, x_lo: 2; x = x_hi * 2 + x_lo), y: 4, z: 8, core: 2. Of those that a mesh axis runs over, the one named last changes fastest.
Arguments:
- concentration: float32 [8, 256, 128, 128], P('size', 'gz'), may hold values from 0 to 2
- deposit: float32 [8, 256, 128, 128], P('size', 'gz'), may hold values from 0 to 1
- velocity: float32 [256, 128, 128], P('gz'), may hold values from 0.2 to 1
- pore_label: int32 [256, 128, 128], P('gz'), may hold values from 0 to 3
- diffusivity: float32 [8], P('size'), may hold values from 0.15 to 0.5
- attach_rate: float32 [8], P('size'), may hold values from 0.4 to 4
- volume: float32 [8], P('size'), may hold values from 0.05 to 0.3
- conc_cotangent: float32 [8, 256, 128, 128], P('size', 'gz'), may hold values from -6 to 6
- deposit_cotangent: float32 [8, 256, 128, 128], P('size', 'gz'), may hold values from -6 to 6
Outputs:
- conc_adjoint: float32 [8, 256, 128, 128], P('size', 'gz')
- deposit_adjoint: float32 [8, 256, 128, 128], P('size', 'gz')
All inputs are finite; a program needn't handle non-finite values.
Results may differ from a plain program's by a relative error of at most 0.0001.
Values sent between devices are 32-bit elements; how exact they have to be, the bound alone decides.
No kernel may reach another device: no remote copies, remote signals or barrier semaphores. Data moves between devices by JAX's collectives and lax.ppermute only.
A program may use at most 64 MiB of HBM per device.

v0:
```python
import jax
import jax.numpy as jnp
from jax import lax
from jax.sharding import PartitionSpec as P

CLOGGING = 1.0
TIME_STEP = 0.25
SURFACE_EFF = (0.1, 0.6, 1.2, 2.0)
MIXING = ((0.0, 1.0), (0.75, 0.25), (1.0 / 3.0, 2.0 / 3.0))


def with_halo(array, sides, width):
    for axis, dim in sides:
        peers, length = (lax.axis_size(axis), array.shape[dim])
        up = [(i, (i + 1) % peers) for i in range(peers - 1)]
        down = [(j, i) for i, j in up]
        last = lax.slice_in_dim(array, length - width, length, axis=dim)
        initial = lax.slice_in_dim(array, 0, width, axis=dim)
        before = lax.ppermute(last, axis, up)
        after = lax.ppermute(initial, axis, down)
        array = jnp.concatenate([before, array, after], axis=dim)
    return array


def efficiency(labels):
    result = jnp.zeros(labels.shape, jnp.float32)
    for label_value in range(4):
        result = result + SURFACE_EFF[label_value] * (labels == label_value).astype(jnp.float32)
    return result


def lateral(extended):
    middle = extended[:, 1:-1]
    padded = jnp.pad(middle, ((0, 0), (0, 0), (1, 1), (1, 1)))
    return (
        extended[:, 2:]
        + extended[:, :-2]
        + padded[:, :, 2:, 1:-1]
        + padded[:, :, :-2, 1:-1]
        + padded[:, :, 1:-1, 2:]
        + padded[:, :, 1:-1, :-2]
        - 6.0 * middle
    )


def shards(
    concentration,
    deposit,
    velocity,
    pore_label,
    diffusivity,
    attach_rate,
    volume,
    conc_cotangent,
    deposit_cotangent,
):
    classes_here = concentration.shape[0]
    coeff_dif = diffusivity[:, None, None, None]
    coeff_rate = attach_rate[:, None, None, None]
    coeff_vol = volume[:, None, None, None]
    collector = efficiency(pore_label)

    def blocking(dep_state):
        partial_sum = jnp.sum(coeff_vol * dep_state, axis=0)
        return jnp.exp(-CLOGGING * lax.psum(partial_sum, "size"))

    def forward_rates(extended, blocked, collect, flow_now):
        middle = extended[:, 1:-1]
        reaction = coeff_rate * collect * blocked * middle
        rate_conc = (
            coeff_dif * lateral(extended) - flow_now * (middle - extended[:, :-2]) - reaction
        )
        return (rate_conc, reaction)

    stacked = jnp.concatenate([concentration, velocity[None]], axis=0)
    first_ext = with_halo(stacked, (("gz", 1),), 1)
    flow_here = first_ext[classes_here, 1:-1]
    flow_above = first_ext[classes_here, 2:]
    blocked_zero = blocking(deposit)
    rate_conc, reaction = forward_rates(
        first_ext[:classes_here], blocked_zero, collector, flow_here
    )
    conc_one = concentration + TIME_STEP * rate_conc
    dep_one = deposit + TIME_STEP * reaction
    blocked_one = blocking(dep_one)
    conc_one_ext = with_halo(conc_one, (("gz", 1),), 1)
    rate_conc, reaction = forward_rates(conc_one_ext, blocked_one, collector, flow_here)
    conc_two = 0.75 * concentration + 0.25 * (conc_one + TIME_STEP * rate_conc)
    dep_two = 0.75 * deposit + 0.25 * (dep_one + TIME_STEP * reaction)
    blocked_two = blocking(dep_two)
    conc_states = (concentration, conc_one, conc_two)
    blocks = (blocked_zero, blocked_one, blocked_two)
    adj_conc = conc_cotangent
    adj_dep = deposit_cotangent
    total_conc = jnp.zeros(concentration.shape, jnp.float32)
    total_dep = jnp.zeros(deposit.shape, jnp.float32)
    for segment_index in (2, 1, 0):
        weight_old, weight_new = MIXING[segment_index]
        push_conc = weight_new * TIME_STEP * adj_conc
        push_ext = with_halo(push_conc, (("gz", 1),), 1)
        uptake = coeff_rate * collector * blocks[segment_index]
        weight = weight_new * TIME_STEP * adj_dep - push_conc
        back_conc = (
            coeff_dif * lateral(push_ext)
            - flow_here * push_conc
            + flow_above * push_ext[:, 2:]
            + uptake * weight
        )
        theta_part = -CLOGGING * jnp.sum(weight * (uptake * conc_states[segment_index]), axis=0)
        theta_grad = lax.psum(theta_part, "size")
        back_conc, back_dep = (back_conc, coeff_vol * theta_grad[None])
        total_conc = total_conc + weight_old * adj_conc
        total_dep = total_dep + weight_old * adj_dep
        adj_conc = weight_new * adj_conc + back_conc
        adj_dep = weight_new * adj_dep + back_dep
    return (total_conc + adj_conc, total_dep + adj_dep)


def solution(mesh):
    in_specs = (
        P("size", "gz", None, None),
        P("size", "gz", None, None),
        P("gz", None, None),
        P("gz", None, None),
        P("size"),
        P("size"),
        P("size"),
        P("size", "gz", None, None),
        P("size", "gz", None, None),
    )
    out_specs = (P("size", "gz", None, None), P("size", "gz", None, None))
    return jax.shard_map(shards, mesh=mesh, in_specs=in_specs, out_specs=out_specs, check_vma=False)
```

profile of v0, /device:TPU:1, one launch (start us, length us, event | category | flops | bytes accessed | tf_op | source)
XLA Modules:
  0.0 333.7 jit_solution(14072504348396859562)
XLA Ops:
  7.2 1.9 multiply_reduce_fusion.4
  9.3 51.8 %all-reduce.12.cloned.1.call-done = f32[4,128,128]{2,1,0:T(8,128)} async-done(((f32[4,128,128]{2,1,0:T(8,128)}), f32[4,128,128]{2,1,0:T(8,128)}) %all-reduce.12.cloned.1.call-update) | async-done | bytes 262160 | tf_op jit(solution)/shard_map/psum | solution.py:65
  64.6 4.0 %collective-permute-start.3 = (f32[3,1,128,128]{3,2,1,0:T(8,128)S(1)}, f32[3,1,128,128]{3,2,1,0:T(8,128)S(1)}, u32[]{:S(2)}, u32[]{:S(2)}) collective-permute-start(f32[3,1,128,128]{3,2,1,0:T(8,128)S(1)} %get-tuple-element.9), channel_id=1, source_target_pairs={{0,1},{1,2},{2,3},{3,4},{4,5},{5,6},{6,7},{7,8},{8,9},{9,10},{10,1... | collective-permute-start | bytes 589832 | tf_op jit(solution)/shard_map/ppermute | solution.py:19
  68.6 42.5 %all-reduce.14.cloned.1.call-done = f32[4,128,128]{2,1,0:T(8,128)} async-done(((f32[4,128,128]{2,1,0:T(8,128)}), f32[4,128,128]{2,1,0:T(8,128)}) %all-reduce.14.cloned.1.call-update) | async-done | bytes 262160 | tf_op jit(solution)/shard_map/psum | solution.py:65
  112.1 1.3 multiply_reduce_fusion.2
  115.5 4.6 %collective-permute-start.7 = (f32[2,1,128,128]{3,2,1,0:T(8,128)}, f32[2,1,128,128]{3,2,1,0:T(8,128)}, u32[]{:S(2)}, u32[]{:S(2)}) collective-permute-start(f32[2,1,128,128]{3,2,1,0:T(8,128)} %get-tuple-element.19), channel_id=1, source_target_pairs={{0,1},{1,2},{2,3},{3,4},{4,5},{5,6},{6,7},{7,8},{8,9},{9,10},{10,1... | collective-permute-start | bytes 393224 | tf_op jit(solution)/shard_map/ppermute | solution.py:19
  120.1 40.9 %all-reduce.16.cloned.1.call-done = f32[4,128,128]{2,1,0:T(8,128)} async-done(((f32[4,128,128]{2,1,0:T(8,128)}), f32[4,128,128]{2,1,0:T(8,128)}) %all-reduce.16.cloned.1.call-update) | async-done | bytes 262160 | tf_op jit(solution)/shard_map/psum | solution.py:65
  162.1 2.4 broadcast_multiply_fusion.2
  166.2 1.3 collective-permute-start
  167.6 4.8 %collective-permute-start.1 = (f32[2,1,128,128]{3,2,1,0:T(8,128)S(1)}, f32[2,1,128,128]{3,2,1,0:T(8,128)}, u32[]{:S(2)}, u32[]{:S(2)}) collective-permute-start(f32[2,1,128,128]{3,2,1,0:T(8,128)S(1)} %get-tuple-element.15), channel_id=1, source_target_pairs={{0,1},{1,2},{2,3},{3,4},{4,5},{5,6},{6,7},{7,8},{8,9},{9,10},{10,1... | collective-permute-start | bytes 393224 | tf_op jit(solution)/shard_map/ppermute | solution.py:19
  174.0 4.2 %collective-permute-done.1 = f32[2,1,128,128]{3,2,1,0:T(8,128)} collective-permute-done((f32[2,1,128,128]{3,2,1,0:T(8,128)S(1)}, f32[2,1,128,128]{3,2,1,0:T(8,128)}, u32[]{:S(2)}, u32[]{:S(2)}) %collective-permute-start.1) | collective-permute-done | bytes 131104 | tf_op jit(solution)/shard_map/ppermute | solution.py:19
  178.2 34.5 %all-reduce.18.cloned.1.call-done = f32[4,128,128]{2,1,0:T(8,128)} async-done(((f32[4,128,128]{2,1,0:T(8,128)}), f32[4,128,128]{2,1,0:T(8,128)}) %all-reduce.18.cloned.1.call-update) | async-done | bytes 262160 | tf_op jit(solution)/shard_map/psum | solution.py:110
  212.8 3.8 %multiply_reduce_fusion.1 = (f32[4,128,128]{2,1,0:T(8,128)S(1)}, f32[2,4,128,128]{3,2,1,0:T(8,128)S(1)}) fusion(f32[2,4,128,128]{3,2,1,0:T(8,128)S(1)} %copy-done.1, f32[2,4,128,128]{3,2,1,0:T(8,128)S(1)} %get-tuple-element.7, f32[4,128,128]{2,1,0:T(8,128)} %all-reduce.18.cloned.1.call-done, f32[4,128,128]{2,1,0:T(8,128)S(1)} %multiply_exponential_fusion.1, ...), kind=kLoop, calls=%fused_computation.110 | loop fusion | flops 3997696 | bytes 4718616 | tf_op jit(solution)/shard_map/reduce_sum | solution.py:109
  218.7 4.6 %collective-permute-start.5 = (f32[2,1,128,128]{3,2,1,0:T(8,128)S(1)}, f32[2,1,128,128]{3,2,1,0:T(8,128)}, u32[]{:S(2)}, u32[]{:S(2)}) collective-permute-start(f32[2,1,128,128]{3,2,1,0:T(8,128)S(1)} %get-tuple-element.13), channel_id=1, source_target_pairs={{0,1},{1,2},{2,3},{3,4},{4,5},{5,6},{6,7},{7,8},{8,9},{9,10},{10,1... | collective-permute-start | bytes 393224 | tf_op jit(solution)/shard_map/ppermute | solution.py:19
  224.3 5.2 %collective-permute-done.5 = f32[2,1,128,128]{3,2,1,0:T(8,128)} collective-permute-done((f32[2,1,128,128]{3,2,1,0:T(8,128)S(1)}, f32[2,1,128,128]{3,2,1,0:T(8,128)}, u32[]{:S(2)}, u32[]{:S(2)}) %collective-permute-start.5) | collective-permute-done | bytes 131104 | tf_op jit(solution)/shard_map/ppermute | solution.py:19
  229.5 34.4 %all-reduce.20.cloned.1.call-done = f32[4,128,128]{2,1,0:T(8,128)} async-done(((f32[4,128,128]{2,1,0:T(8,128)}), f32[4,128,128]{2,1,0:T(8,128)}) %all-reduce.20.cloned.1.call-update) | async-done | bytes 262160 | tf_op jit(solution)/shard_map/psum | solution.py:110
  263.8 3.8 %multiply_reduce_fusion = (f32[4,128,128]{2,1,0:T(8,128)S(1)}, f32[2,4,128,128]{3,2,1,0:T(8,128)S(1)}) fusion(f32[2,4,128,128]{3,2,1,0:T(8,128)S(1)} %copy-done.1, f32[2,4,128,128]{3,2,1,0:T(8,128)S(1)} %copy-done, f32[4,128,128]{2,1,0:T(8,128)} %all-reduce.20.cloned.1.call-done, f32[4,128,128]{2,1,0:T(8,128)} %all-reduce.18.cloned.1.call-done, ...), kind=kLoop, calls=%fused_computation.107 | loop fusion | flops 4521984 | bytes 4980760 | tf_op jit(solution)/shard_map/reduce_sum | solution.py:109
  268.4 1.7 fusion.74
  270.1 1.4 collective-permute-start.8
  271.5 4.6 %collective-permute-start.9 = (f32[2,1,128,128]{3,2,1,0:T(8,128)}, f32[2,1,128,128]{3,2,1,0:T(8,128)}, u32[]{:S(2)}, u32[]{:S(2)}) collective-permute-start(f32[2,1,128,128]{3,2,1,0:T(8,128)} %get-tuple-element.11), channel_id=1, source_target_pairs={{0,1},{1,2},{2,3},{3,4},{4,5},{5,6},{6,7},{7,8},{8,9},{9,10},{10,1... | collective-permute-start | bytes 393224 | tf_op jit(solution)/shard_map/ppermute | solution.py:19
  277.3 4.6 %collective-permute-done.9 = f32[2,1,128,128]{3,2,1,0:T(8,128)} collective-permute-done((f32[2,1,128,128]{3,2,1,0:T(8,128)}, f32[2,1,128,128]{3,2,1,0:T(8,128)}, u32[]{:S(2)}, u32[]{:S(2)}) %collective-permute-start.9) | collective-permute-done | bytes 131104 | tf_op jit(solution)/shard_map/ppermute | solution.py:19
  281.9 4.4 %fusion.14 = f32[2,4,128,128]{3,2,1,0:T(8,128)} fusion(f32[2,4,128,128]{3,2,1,0:T(8,128)S(1)} %get-tuple-element.3, f32[2,4,128,128]{3,2,1,0:T(8,128)} %broadcast_multiply_fusion.1, f32[2,1,128,128]{3,2,1,0:T(8,128)} %collective-permute-done.9, f32[2,1,128,128]{3,2,1,0:T(8,128)S(1)} %collective-permute-done.8, f32[2,4,128,128]{3,2,1,0:T(8,128)S(1)} %get-tuple-element.5, ...), kind=kLoop, calls=%fused_computation.37 | loop fusion | flops 4325376 | bytes 4980760 | tf_op jit(solution)/shard_map/add | solution.py:116
  286.3 38.6 %all-reduce.22.cloned.1.call-done = f32[4,128,128]{2,1,0:T(8,128)} async-done(((f32[4,128,128]{2,1,0:T(8,128)}), f32[4,128,128]{2,1,0:T(8,128)}) %all-reduce.22.cloned.1.call-update) | async-done | bytes 262160 | tf_op jit(solution)/shard_map/psum | solution.py:110
  324.8 2.0 add_add_fusion
  (70 shorter events, 16.0 us)
Async XLA Ops:
  7.2 54.0 %all-reduce.12.cloned.1.call-start = ((), (), s32[]{:S(2)}) async-start(), calls=%async_computation | async-start | bytes 524288 | tf_op jit(solution)/shard_map/psum | solution.py:65
  9.1 53.0 %copy-start.13 = (f32[2]{0:T(128)S(1)}, f32[2]{0:T(128)}, u32[]{:S(2)}) copy-start(f32[2]{0:T(128)} %param.15) | copy-start | bytes 28
  9.1 53.0 %copy-start.14 = (f32[2]{0:T(128)S(1)}, f32[2]{0:T(128)}, u32[]{:S(2)}) copy-start(f32[2]{0:T(128)} %param.14) | copy-start | bytes 28
  9.2 53.0 %copy-start = (f32[2,4,128,128]{3,2,1,0:T(8,128)S(1)}, f32[2,4,128,128]{3,2,1,0:T(8,128)}, u32[]{:S(2)}) copy-start(f32[2,4,128,128]{3,2,1,0:T(8,128)} %param.9) | copy-start | bytes 1572868
  9.2 53.0 %copy-start.3 = (f32[2,4,128,128]{3,2,1,0:T(8,128)S(1)}, f32[2,4,128,128]{3,2,1,0:T(8,128)}, u32[]{:S(2)}) copy-start(f32[2,4,128,128]{3,2,1,0:T(8,128)} %param.10) | copy-start | bytes 1572868
  9.2 101.9 %all-reduce.14.cloned.1.call-start = ((), (), s32[]{:S(2)}) async-start(), calls=%async_computation.1 | async-start | bytes 524288 | tf_op jit(solution)/shard_map/psum | solution.py:65
  63.2 97.9 %all-reduce.16.cloned.1.call-start = ((), (), s32[]{:S(2)}) async-start(), calls=%async_computation.2 | async-start | bytes 524288 | tf_op jit(solution)/shard_map/psum | solution.py:65
  63.2 48.8 %copy-start.15 = (f32[2]{0:T(128)S(1)}, f32[2]{0:T(128)}, u32[]{:S(2)}) copy-start(f32[2]{0:T(128)} %param.13) | copy-start | bytes 28
  63.3 48.8 %collective-permute-start.2 = (f32[3,1,128,128]{3,2,1,0:T(8,128)S(1)}, f32[3,1,128,128]{3,2,1,0:T(8,128)S(1)}, u32[]{:S(2)}, u32[]{:S(2)}) collective-permute-start(f32[3,1,128,128]{3,2,1,0:T(8,128)S(1)} %get-tuple-element.8), channel_id=1, source_target_pairs={{1,0},{2,1},{3,2},{4,3},{5,4},{6,5},{7,6},{8,7},{9,8},{10,9},{11,1... | collective-permute-start | bytes 589832 | tf_op jit(solution)/shard_map/ppermute | solution.py:20
  64.6 47.5 %collective-permute-start.3 = (f32[3,1,128,128]{3,2,1,0:T(8,128)S(1)}, f32[3,1,128,128]{3,2,1,0:T(8,128)S(1)}, u32[]{:S(2)}, u32[]{:S(2)}) collective-permute-start(f32[3,1,128,128]{3,2,1,0:T(8,128)S(1)} %get-tuple-element.9), channel_id=1, source_target_pairs={{0,1},{1,2},{2,3},{3,4},{4,5},{5,6},{6,7},{7,8},{8,9},{9,10},{10,1... | collective-permute-start | bytes 589832 | tf_op jit(solution)/shard_map/ppermute | solution.py:19
  113.4 99.3 %all-reduce.18.cloned.1.call-start = ((), (), s32[]{:S(2)}) async-start(), calls=%async_computation.3 | async-start | bytes 524288 | tf_op jit(solution)/shard_map/psum | solution.py:110
  113.5 48.6 %copy-start.1 = (f32[2,4,128,128]{3,2,1,0:T(8,128)S(1)}, f32[2,4,128,128]{3,2,1,0:T(8,128)}, u32[]{:S(2)}) copy-start(f32[2,4,128,128]{3,2,1,0:T(8,128)} %param.17) | copy-start | bytes 1572868
  113.5 48.6 %copy-start.4 = (f32[2,4,128,128]{3,2,1,0:T(8,128)S(1)}, f32[2,4,128,128]{3,2,1,0:T(8,128)}, u32[]{:S(2)}) copy-start(f32[2,4,128,128]{3,2,1,0:T(8,128)} %param.16) | copy-start | bytes 1572868
  114.2 47.8 %collective-permute-start.6 = (f32[2,1,128,128]{3,2,1,0:T(8,128)}, f32[2,1,128,128]{3,2,1,0:T(8,128)S(1)}, u32[]{:S(2)}, u32[]{:S(2)}) collective-permute-start(f32[2,1,128,128]{3,2,1,0:T(8,128)} %get-tuple-element.18), channel_id=1, source_target_pairs={{1,0},{2,1},{3,2},{4,3},{5,4},{6,5},{7,6},{8,7},{9,8},{10,9},{11,1... | collective-permute-start | bytes 393224 | tf_op jit(solution)/shard_map/ppermute | solution.py:20
  115.5 46.5 %collective-permute-start.7 = (f32[2,1,128,128]{3,2,1,0:T(8,128)}, f32[2,1,128,128]{3,2,1,0:T(8,128)}, u32[]{:S(2)}, u32[]{:S(2)}) collective-permute-start(f32[2,1,128,128]{3,2,1,0:T(8,128)} %get-tuple-element.19), channel_id=1, source_target_pairs={{0,1},{1,2},{2,3},{3,4},{4,5},{5,6},{6,7},{7,8},{8,9},{9,10},{10,1... | collective-permute-start | bytes 393224 | tf_op jit(solution)/shard_map/ppermute | solution.py:19
  165.2 98.6 %all-reduce.20.cloned.1.call-start = ((), (), s32[]{:S(2)}) async-start(), calls=%async_computation.4 | async-start | bytes 524288 | tf_op jit(solution)/shard_map/psum | solution.py:110
  166.2 7.8 %collective-permute-start = (f32[2,1,128,128]{3,2,1,0:T(8,128)S(1)}, f32[2,1,128,128]{3,2,1,0:T(8,128)S(1)}, u32[]{:S(2)}, u32[]{:S(2)}) collective-permute-start(f32[2,1,128,128]{3,2,1,0:T(8,128)S(1)} %get-tuple-element.14), channel_id=1, source_target_pairs={{1,0},{2,1},{3,2},{4,3},{5,4},{6,5},{7,6},{8,7},{9,8},{10,9},{11,1... | collective-permute-start | bytes 393224 | tf_op jit(solution)/shard_map/ppermute | solution.py:20
  167.6 10.7 %collective-permute-start.1 = (f32[2,1,128,128]{3,2,1,0:T(8,128)S(1)}, f32[2,1,128,128]{3,2,1,0:T(8,128)}, u32[]{:S(2)}, u32[]{:S(2)}) collective-permute-start(f32[2,1,128,128]{3,2,1,0:T(8,128)S(1)} %get-tuple-element.15), channel_id=1, source_target_pairs={{0,1},{1,2},{2,3},{3,4},{4,5},{5,6},{6,7},{7,8},{8,9},{9,10},{10,1... | collective-permute-start | bytes 393224 | tf_op jit(solution)/shard_map/ppermute | solution.py:19
  217.3 107.5 %all-reduce.22.cloned.1.call-start = ((), (), s32[]{:S(2)}) async-start(), calls=%async_computation.5 | async-start | bytes 524288 | tf_op jit(solution)/shard_map/psum | solution.py:110
  217.4 46.4 %copy-start.7 = (f32[2,4,128,128]{3,2,1,0:T(8,128)}, f32[2,4,128,128]{3,2,1,0:T(8,128)S(1)}, u32[]{:S(2)}) copy-start(f32[2,4,128,128]{3,2,1,0:T(8,128)S(1)} %broadcast_multiply_fusion) | copy-start | bytes 1572868
  217.4 6.8 %collective-permute-start.4 = (f32[2,1,128,128]{3,2,1,0:T(8,128)S(1)}, f32[2,1,128,128]{3,2,1,0:T(8,128)S(1)}, u32[]{:S(2)}, u32[]{:S(2)}) collective-permute-start(f32[2,1,128,128]{3,2,1,0:T(8,128)S(1)} %get-tuple-element.12), channel_id=1, source_target_pairs={{1,0},{2,1},{3,2},{4,3},{5,4},{6,5},{7,6},{8,7},{9,8},{10,9},{11,1... | collective-permute-start | bytes 393224 | tf_op jit(solution)/shard_map/ppermute | solution.py:20
  218.7 10.7 %collective-permute-start.5 = (f32[2,1,128,128]{3,2,1,0:T(8,128)S(1)}, f32[2,1,128,128]{3,2,1,0:T(8,128)}, u32[]{:S(2)}, u32[]{:S(2)}) collective-permute-start(f32[2,1,128,128]{3,2,1,0:T(8,128)S(1)} %get-tuple-element.13), channel_id=1, source_target_pairs={{0,1},{1,2},{2,3},{3,4},{4,5},{5,6},{6,7},{7,8},{8,9},{9,10},{10,1... | collective-permute-start | bytes 393224 | tf_op jit(solution)/shard_map/ppermute | solution.py:19
  270.1 7.2 %collective-permute-start.8 = (f32[2,1,128,128]{3,2,1,0:T(8,128)}, f32[2,1,128,128]{3,2,1,0:T(8,128)S(1)}, u32[]{:S(2)}, u32[]{:S(2)}) collective-permute-start(f32[2,1,128,128]{3,2,1,0:T(8,128)} %get-tuple-element.10), channel_id=1, source_target_pairs={{1,0},{2,1},{3,2},{4,3},{5,4},{6,5},{7,6},{8,7},{9,8},{10,9},{11,1... | collective-permute-start | bytes 393224 | tf_op jit(solution)/shard_map/ppermute | solution.py:20
  271.5 10.3 %collective-permute-start.9 = (f32[2,1,128,128]{3,2,1,0:T(8,128)}, f32[2,1,128,128]{3,2,1,0:T(8,128)}, u32[]{:S(2)}, u32[]{:S(2)}) collective-permute-start(f32[2,1,128,128]{3,2,1,0:T(8,128)} %get-tuple-element.11), channel_id=1, source_target_pairs={{0,1},{1,2},{2,3},{3,4},{4,5},{5,6},{6,7},{7,8},{8,9},{9,10},{10,1... | collective-permute-start | bytes 393224 | tf_op jit(solution)/shard_map/ppermute | solution.py:19
  (8 other events, 47.8 us)
Sparse Core Ops, SparseCore 0:
  11.2 49.9 all-reduce.11
  64.6 46.4 all-reduce.13
  114.2 46.7 all-reduce.15
  165.3 47.3 all-reduce.17
  217.4 46.3 all-reduce.19
  277.0 47.7 all-reduce.21
where the time goes:
time: 334 us
  waiting for transfers between devices  258 us (77%)
  starting transfers between devices  29.5 us (9%)
  other arithmetic  28.3 us (8%)
  between operations  14.4 us (4%)
  local copies, waits for them, and re-layouts  3.47 us (1%)
    psum x3, waiting for transfers between devices, blocking(): return jnp.exp(-CLOGGING * lax.psum(partial_sum, 'size'))  135 us
    psum x3, waiting for transfers between devices, shards(): theta_grad = lax.psum(theta_part, 'size')  107 us
    ppermute x5, starting transfers between devices, with_halo(): before = lax.ppermute(last, axis, up)  22.7 us
    ppermute x5, waiting for transfers between devices, with_halo(): before = lax.ppermute(last, axis, up)  14 us
    reduce_sum x2, other arithmetic, shards(): jnp.sum(weight * (uptake * conc_states[segment_index]), axis=0)  7.57 us
  transfers between devices with their start and end apart: 16, of which 11 were waited for; matrix products, arithmetic and copies ran while one was open for 3% of the time, Pallas kernels for 0%

commit v1 on v0

--- a/solution.py
+++ b/solution.py
@@ -107,7 +107,7 @@
             + uptake * weight
         )
         theta_part = -CLOGGING * jnp.sum(weight * (uptake * conc_states[segment_index]), axis=0)
-        theta_grad = lax.psum(theta_part, "size")
+        theta_grad = jnp.sum(lax.all_gather(theta_part, "size"), axis=0)
         back_conc, back_dep = (back_conc, coeff_vol * theta_grad[None])
         total_conc = total_conc + weight_old * adj_conc
         total_dep = total_dep + weight_old * adj_dep

time: 334 us -> 257 us (0.77)
  waiting for transfers between devices: 258 us -> 183 us
    psum x3 -> x0, waiting for transfers between devices: 107 us -> none  [shards(): theta_grad = lax.psum(theta_part, 'size')]
    all_gather x0 -> x3, waiting for transfers between devices: none -> 42 us  [shards(): theta_grad = jnp.sum(lax.all_gather(theta_part, 'size'), axis=0)]
    ppermute x5, waiting for transfers between devices: 14 us -> 4.59 us  [with_halo(): before = lax.ppermute(last, axis, up)]
    reduce_sum x0 -> x3, other arithmetic: none -> 4.62 us  [shards(): theta_grad = jnp.sum(lax.all_gather(theta_part, 'size'), axis=0)]
    add x2, other arithmetic: 6.45 us -> 2.58 us  [shards(): return (total_conc + adj_conc, total_dep + adj_dep)]
  transfers between devices with their start and end apart: 16 -> 16, of which waited for: 11 -> 8; matrix products, arithmetic and copies ran while one was open for 3% -> 4% of each run, Pallas kernels for 0% -> 0%
where the time goes in v1:
time: 257 us
  waiting for transfers between devices  183 us (71%)
  starting transfers between devices  28.1 us (11%)
  other arithmetic  26.7 us (10%)
  between operations  14.5 us (6%)
  local copies, waits for them, and re-layouts  3.89 us (2%)
    psum x3, waiting for transfers between devices, blocking(): return jnp.exp(-CLOGGING * lax.psum(partial_sum, 'size'))  135 us
    all_gather x3, waiting for transfers between devices, shards(): theta_grad = jnp.sum(lax.all_gather(theta_part, 'size'), axis=0)  42 us
    ppermute x5, starting transfers between devices, with_halo(): before = lax.ppermute(last, axis, up)  21.3 us
    reduce_sum x2, other arithmetic, shards(): jnp.sum(weight * (uptake * conc_states[segment_index]), axis=0)  6.61 us
    ppermute x5, starting transfers between devices, with_halo(): after = lax.ppermute(initial, axis, down)  6.56 us
  transfers between devices with their start and end apart: 16, of which 8 were waited for; matrix products, arithmetic and copies ran while one was open for 4% of the time, Pallas kernels for 0%

profile of v1, /device:TPU:1, one launch (start us, length us, event | category | flops | bytes accessed | tf_op | source)
XLA Modules:
  0.0 256.6 jit_solution(6503182846273364786)
XLA Ops:
  7.3 2.0 multiply_reduce_fusion.4
  9.4 51.8 %all-reduce.9.cloned.1.call-done = f32[4,128,128]{2,1,0:T(8,128)} async-done(((f32[4,128,128]{2,1,0:T(8,128)}), f32[4,128,128]{2,1,0:T(8,128)}) %all-reduce.9.cloned.1.call-update) | async-done | bytes 262160 | tf_op jit(solution)/shard_map/psum | solution.py:65
  64.6 4.0 %collective-permute-start.3 = (f32[3,1,128,128]{3,2,1,0:T(8,128)S(1)}, f32[3,1,128,128]{3,2,1,0:T(8,128)S(1)}, u32[]{:S(2)}, u32[]{:S(2)}) collective-permute-start(f32[3,1,128,128]{3,2,1,0:T(8,128)S(1)} %get-tuple-element.9), channel_id=1, source_target_pairs={{0,1},{1,2},{2,3},{3,4},{4,5},{5,6},{6,7},{7,8},{8,9},{9,10},{10,1... | collective-permute-start | bytes 589832 | tf_op jit(solution)/shard_map/ppermute | solution.py:19
  68.6 42.7 %all-reduce.11.cloned.1.call-done = f32[4,128,128]{2,1,0:T(8,128)} async-done(((f32[4,128,128]{2,1,0:T(8,128)}), f32[4,128,128]{2,1,0:T(8,128)}) %all-reduce.11.cloned.1.call-update) | async-done | bytes 262160 | tf_op jit(solution)/shard_map/psum | solution.py:65
  112.3 1.3 multiply_reduce_fusion.2
  115.8 4.6 %collective-permute-start.7 = (f32[2,1,128,128]{3,2,1,0:T(8,128)}, f32[2,1,128,128]{3,2,1,0:T(8,128)}, u32[]{:S(2)}, u32[]{:S(2)}) collective-permute-start(f32[2,1,128,128]{3,2,1,0:T(8,128)} %get-tuple-element.19), channel_id=1, source_target_pairs={{0,1},{1,2},{2,3},{3,4},{4,5},{5,6},{6,7},{7,8},{8,9},{9,10},{10,1... | collective-permute-start | bytes 393224 | tf_op jit(solution)/shard_map/ppermute | solution.py:19
  120.4 40.9 %all-reduce.13.cloned.1.call-done = f32[4,128,128]{2,1,0:T(8,128)} async-done(((f32[4,128,128]{2,1,0:T(8,128)}), f32[4,128,128]{2,1,0:T(8,128)}) %all-reduce.13.cloned.1.call-update) | async-done | bytes 262160 | tf_op jit(solution)/shard_map/psum | solution.py:65
  162.3 2.4 broadcast_multiply_fusion.2
  165.5 1.7 fusion.76
  168.4 4.0 %collective-permute-start.1 = (f32[2,1,128,128]{3,2,1,0:T(8,128)S(1)}, f32[2,1,128,128]{3,2,1,0:T(8,128)S(1)}, u32[]{:S(2)}, u32[]{:S(2)}) collective-permute-start(f32[2,1,128,128]{3,2,1,0:T(8,128)S(1)} %get-tuple-element.15), channel_id=1, source_target_pairs={{0,1},{1,2},{2,3},{3,4},{4,5},{5,6},{6,7},{7,8},{8,9},{9,10},{10,1... | collective-permute-start | bytes 393224 | tf_op jit(solution)/shard_map/ppermute | solution.py:19
  173.4 14.9 %all-gather.7.cloned.1.call-done = f32[16,128,128]{2,1,0:T(8,128)} async-done(((f32[4,128,128]{2,1,0:T(8,128)}), f32[16,128,128]{2,1,0:T(8,128)}) %all-gather.7.cloned.1.call-update) | async-done | bytes 1048592 | tf_op jit(solution)/shard_map/all_gather | solution.py:110
  188.3 1.3 reduce_sum.85
  190.3 3.4 %multiply_reduce_fusion.1 = (f32[4,128,128]{2,1,0:T(8,128)S(1)}, f32[2,4,128,128]{3,2,1,0:T(8,128)S(1)}) fusion(f32[2,4,128,128]{3,2,1,0:T(8,128)S(1)} %copy-done.1, f32[2,4,128,128]{3,2,1,0:T(8,128)S(1)} %get-tuple-element.7, f32[4,128,128]{2,1,0:T(8,128)S(1)} %reduce_sum.85, f32[4,128,128]{2,1,0:T(8,128)S(1)} %multiply_exponential_fusion.1, ...), kind=kLoop, calls=%fused_computation.110 | loop fusion | flops 3997696 | bytes 4718616 | tf_op jit(solution)/shard_map/reduce_sum | solution.py:109
  196.6 4.6 %collective-permute-start.5 = (f32[2,1,128,128]{3,2,1,0:T(8,128)}, f32[2,1,128,128]{3,2,1,0:T(8,128)}, u32[]{:S(2)}, u32[]{:S(2)}) collective-permute-start(f32[2,1,128,128]{3,2,1,0:T(8,128)} %get-tuple-element.13), channel_id=1, source_target_pairs={{0,1},{1,2},{2,3},{3,4},{4,5},{5,6},{6,7},{7,8},{8,9},{9,10},{10,1... | collective-permute-start | bytes 393224 | tf_op jit(solution)/shard_map/ppermute | solution.py:19
  201.2 17.2 %all-gather.9.cloned.1.call-done = f32[16,128,128]{2,1,0:T(8,128)} async-done(((f32[4,128,128]{2,1,0:T(8,128)}), f32[16,128,128]{2,1,0:T(8,128)}) %all-gather.9.cloned.1.call-update) | async-done | bytes 1048592 | tf_op jit(solution)/shard_map/all_gather | solution.py:110
  218.4 2.0 reduce_sum.87
  220.4 3.2 %multiply_reduce_fusion = (f32[4,128,128]{2,1,0:T(8,128)S(1)}, f32[2,4,128,128]{3,2,1,0:T(8,128)S(1)}) fusion(f32[2,4,128,128]{3,2,1,0:T(8,128)S(1)} %copy-done.1, f32[2,4,128,128]{3,2,1,0:T(8,128)S(1)} %copy-done, f32[4,128,128]{2,1,0:T(8,128)} %reduce_sum.87, f32[4,128,128]{2,1,0:T(8,128)S(1)} %reduce_sum.85, ...), kind=kLoop, calls=%fused_computation.107 | loop fusion | flops 4521984 | bytes 4980760 | tf_op jit(solution)/shard_map/reduce_sum | solution.py:109
  224.5 1.4 collective-permute-start.8
  225.9 4.0 %collective-permute-start.9 = (f32[2,1,128,128]{3,2,1,0:T(8,128)S(1)}, f32[2,1,128,128]{3,2,1,0:T(8,128)S(1)}, u32[]{:S(2)}, u32[]{:S(2)}) collective-permute-start(f32[2,1,128,128]{3,2,1,0:T(8,128)S(1)} %get-tuple-element.11), channel_id=1, source_target_pairs={{0,1},{1,2},{2,3},{3,4},{4,5},{5,6},{6,7},{7,8},{8,9},{9,10},{10,1... | collective-permute-start | bytes 393224 | tf_op jit(solution)/shard_map/ppermute | solution.py:19
  229.9 1.4 collective-permute-done.8
  231.3 4.6 %collective-permute-done.9 = f32[2,1,128,128]{3,2,1,0:T(8,128)S(1)} collective-permute-done((f32[2,1,128,128]{3,2,1,0:T(8,128)S(1)}, f32[2,1,128,128]{3,2,1,0:T(8,128)S(1)}, u32[]{:S(2)}, u32[]{:S(2)}) %collective-permute-start.9) | collective-permute-done | bytes 131104 | tf_op jit(solution)/shard_map/ppermute | solution.py:19
  235.9 1.5 fusion.14
  237.4 10.0 %all-gather.11.cloned.1.call-done = f32[16,128,128]{2,1,0:T(8,128)} async-done(((f32[4,128,128]{2,1,0:T(8,128)}), f32[16,128,128]{2,1,0:T(8,128)}) %all-gather.11.cloned.1.call-update) | async-done | bytes 1048592 | tf_op jit(solution)/shard_map/all_gather | solution.py:110
  247.3 1.3 reduce_sum.89
  (75 shorter events, 16.1 us)
Async XLA Ops:
  7.2 55.0 %copy-start.14 = (f32[2]{0:T(128)S(1)}, f32[2]{0:T(128)}, u32[]{:S(2)}) copy-start(f32[2]{0:T(128)} %param.15) | copy-start | bytes 28
  7.2 55.0 %copy-start.3 = (f32[2,4,128,128]{3,2,1,0:T(8,128)S(1)}, f32[2,4,128,128]{3,2,1,0:T(8,128)}, u32[]{:S(2)}) copy-start(f32[2,4,128,128]{3,2,1,0:T(8,128)} %param.10) | copy-start | bytes 1572868
  7.2 55.0 %copy-start.15 = (f32[2]{0:T(128)S(1)}, f32[2]{0:T(128)}, u32[]{:S(2)}) copy-start(f32[2]{0:T(128)} %param.14) | copy-start | bytes 28
  7.2 55.0 %copy-start = (f32[2,4,128,128]{3,2,1,0:T(8,128)S(1)}, f32[2,4,128,128]{3,2,1,0:T(8,128)}, u32[]{:S(2)}) copy-start(f32[2,4,128,128]{3,2,1,0:T(8,128)} %param.9) | copy-start | bytes 1572868
  7.2 54.0 %all-reduce.9.cloned.1.call-start = ((), (), s32[]{:S(2)}) async-start(), calls=%async_computation | async-start | bytes 524288 | tf_op jit(solution)/shard_map/psum | solution.py:65
  9.2 102.1 %all-reduce.11.cloned.1.call-start = ((), (), s32[]{:S(2)}) async-start(), calls=%async_computation.1 | async-start | bytes 524288 | tf_op jit(solution)/shard_map/psum | solution.py:65
  63.2 49.2 %copy-start.16 = (f32[2]{0:T(128)S(1)}, f32[2]{0:T(128)}, u32[]{:S(2)}) copy-start(f32[2]{0:T(128)} %param.13) | copy-start | bytes 28
  63.2 98.1 %all-reduce.13.cloned.1.call-start = ((), (), s32[]{:S(2)}) async-start(), calls=%async_computation.2 | async-start | bytes 524288 | tf_op jit(solution)/shard_map/psum | solution.py:65
  63.3 49.0 %collective-permute-start.2 = (f32[3,1,128,128]{3,2,1,0:T(8,128)S(1)}, f32[3,1,128,128]{3,2,1,0:T(8,128)S(1)}, u32[]{:S(2)}, u32[]{:S(2)}) collective-permute-start(f32[3,1,128,128]{3,2,1,0:T(8,128)S(1)} %get-tuple-element.8), channel_id=1, source_target_pairs={{1,0},{2,1},{3,2},{4,3},{5,4},{6,5},{7,6},{8,7},{9,8},{10,9},{11,1... | collective-permute-start | bytes 589832 | tf_op jit(solution)/shard_map/ppermute | solution.py:20
  64.6 47.7 %collective-permute-start.3 = (f32[3,1,128,128]{3,2,1,0:T(8,128)S(1)}, f32[3,1,128,128]{3,2,1,0:T(8,128)S(1)}, u32[]{:S(2)}, u32[]{:S(2)}) collective-permute-start(f32[3,1,128,128]{3,2,1,0:T(8,128)S(1)} %get-tuple-element.9), channel_id=1, source_target_pairs={{0,1},{1,2},{2,3},{3,4},{4,5},{5,6},{6,7},{7,8},{8,9},{9,10},{10,1... | collective-permute-start | bytes 589832 | tf_op jit(solution)/shard_map/ppermute | solution.py:19
  113.7 48.6 %copy-start.1 = (f32[2,4,128,128]{3,2,1,0:T(8,128)S(1)}, f32[2,4,128,128]{3,2,1,0:T(8,128)}, u32[]{:S(2)}) copy-start(f32[2,4,128,128]{3,2,1,0:T(8,128)} %param.17) | copy-start | bytes 1572868
  113.7 48.6 %copy-start.4 = (f32[2,4,128,128]{3,2,1,0:T(8,128)S(1)}, f32[2,4,128,128]{3,2,1,0:T(8,128)}, u32[]{:S(2)}) copy-start(f32[2,4,128,128]{3,2,1,0:T(8,128)} %param.16) | copy-start | bytes 1572868
  113.7 74.6 %all-gather.7.cloned.1.call-start = ((), (), s32[]{:S(2)}) async-start(), calls=%async_computation.3 | async-start | bytes 1310720 | tf_op jit(solution)/shard_map/all_gather | solution.py:110
  114.5 47.8 %collective-permute-start.6 = (f32[2,1,128,128]{3,2,1,0:T(8,128)}, f32[2,1,128,128]{3,2,1,0:T(8,128)S(1)}, u32[]{:S(2)}, u32[]{:S(2)}) collective-permute-start(f32[2,1,128,128]{3,2,1,0:T(8,128)} %get-tuple-element.18), channel_id=1, source_target_pairs={{1,0},{2,1},{3,2},{4,3},{5,4},{6,5},{7,6},{8,7},{9,8},{10,9},{11,1... | collective-permute-start | bytes 393224 | tf_op jit(solution)/shard_map/ppermute | solution.py:20
  115.8 46.5 %collective-permute-start.7 = (f32[2,1,128,128]{3,2,1,0:T(8,128)}, f32[2,1,128,128]{3,2,1,0:T(8,128)}, u32[]{:S(2)}, u32[]{:S(2)}) collective-permute-start(f32[2,1,128,128]{3,2,1,0:T(8,128)} %get-tuple-element.19), channel_id=1, source_target_pairs={{0,1},{1,2},{2,3},{3,4},{4,5},{5,6},{6,7},{7,8},{8,9},{9,10},{10,1... | collective-permute-start | bytes 393224 | tf_op jit(solution)/shard_map/ppermute | solution.py:19
  165.4 53.0 %all-gather.9.cloned.1.call-start = ((), (), s32[]{:S(2)}) async-start(), calls=%async_computation.4 | async-start | bytes 1310720 | tf_op jit(solution)/shard_map/all_gather | solution.py:110
  167.1 22.5 %collective-permute-start = (f32[2,1,128,128]{3,2,1,0:T(8,128)}, f32[2,1,128,128]{3,2,1,0:T(8,128)S(1)}, u32[]{:S(2)}, u32[]{:S(2)}) collective-permute-start(f32[2,1,128,128]{3,2,1,0:T(8,128)} %get-tuple-element.14), channel_id=1, source_target_pairs={{1,0},{2,1},{3,2},{4,3},{5,4},{6,5},{7,6},{8,7},{9,8},{10,9},{11,1... | collective-permute-start | bytes 393224 | tf_op jit(solution)/shard_map/ppermute | solution.py:20
  168.4 21.2 %collective-permute-start.1 = (f32[2,1,128,128]{3,2,1,0:T(8,128)S(1)}, f32[2,1,128,128]{3,2,1,0:T(8,128)S(1)}, u32[]{:S(2)}, u32[]{:S(2)}) collective-permute-start(f32[2,1,128,128]{3,2,1,0:T(8,128)S(1)} %get-tuple-element.15), channel_id=1, source_target_pairs={{0,1},{1,2},{2,3},{3,4},{4,5},{5,6},{6,7},{7,8},{8,9},{9,10},{10,1... | collective-permute-start | bytes 393224 | tf_op jit(solution)/shard_map/ppermute | solution.py:19
  194.4 52.9 %all-gather.11.cloned.1.call-start = ((), (), s32[]{:S(2)}) async-start(), calls=%async_computation.5 | async-start | bytes 1310720 | tf_op jit(solution)/shard_map/all_gather | solution.py:110
  194.5 25.9 %copy-start.7 = (f32[2,4,128,128]{3,2,1,0:T(8,128)}, f32[2,4,128,128]{3,2,1,0:T(8,128)S(1)}, u32[]{:S(2)}) copy-start(f32[2,4,128,128]{3,2,1,0:T(8,128)S(1)} %broadcast_multiply_fusion) | copy-start | bytes 1572868
  195.3 25.1 %collective-permute-start.4 = (f32[2,1,128,128]{3,2,1,0:T(8,128)}, f32[2,1,128,128]{3,2,1,0:T(8,128)S(1)}, u32[]{:S(2)}, u32[]{:S(2)}) collective-permute-start(f32[2,1,128,128]{3,2,1,0:T(8,128)} %get-tuple-element.12), channel_id=1, source_target_pairs={{1,0},{2,1},{3,2},{4,3},{5,4},{6,5},{7,6},{8,7},{9,8},{10,9},{11,1... | collective-permute-start | bytes 393224 | tf_op jit(solution)/shard_map/ppermute | solution.py:20
  196.6 23.8 %collective-permute-start.5 = (f32[2,1,128,128]{3,2,1,0:T(8,128)}, f32[2,1,128,128]{3,2,1,0:T(8,128)}, u32[]{:S(2)}, u32[]{:S(2)}) collective-permute-start(f32[2,1,128,128]{3,2,1,0:T(8,128)} %get-tuple-element.13), channel_id=1, source_target_pairs={{0,1},{1,2},{2,3},{3,4},{4,5},{5,6},{6,7},{7,8},{8,9},{9,10},{10,1... | collective-permute-start | bytes 393224 | tf_op jit(solution)/shard_map/ppermute | solution.py:19
  224.5 6.8 %collective-permute-start.8 = (f32[2,1,128,128]{3,2,1,0:T(8,128)S(1)}, f32[2,1,128,128]{3,2,1,0:T(8,128)S(1)}, u32[]{:S(2)}, u32[]{:S(2)}) collective-permute-start(f32[2,1,128,128]{3,2,1,0:T(8,128)S(1)} %get-tuple-element.10), channel_id=1, source_target_pairs={{1,0},{2,1},{3,2},{4,3},{5,4},{6,5},{7,6},{8,7},{9,8},{10,9},{11,1... | collective-permute-start | bytes 393224 | tf_op jit(solution)/shard_map/ppermute | solution.py:20
  225.9 10.0 %collective-permute-start.9 = (f32[2,1,128,128]{3,2,1,0:T(8,128)S(1)}, f32[2,1,128,128]{3,2,1,0:T(8,128)S(1)}, u32[]{:S(2)}, u32[]{:S(2)}) collective-permute-start(f32[2,1,128,128]{3,2,1,0:T(8,128)S(1)} %get-tuple-element.11), channel_id=1, source_target_pairs={{0,1},{1,2},{2,3},{3,4},{4,5},{5,6},{6,7},{7,8},{8,9},{9,10},{10,1... | collective-permute-start | bytes 393224 | tf_op jit(solution)/shard_map/ppermute | solution.py:19
  (9 other events, 50.1 us)
Sparse Core Ops, SparseCore 0:
  11.3 49.9 all-reduce.8
  64.6 46.6 all-reduce.10
  114.5 46.7 all-reduce.12
  165.6 22.6 all-gather.6
  194.5 23.8 all-gather.8
  224.5 22.7 all-gather.10
